TPU v7x, 768 devices: a whole 4x8x12 slice. The times are simulated.
768 devices in a mesh: wide: 32 (over z_lo, y), rep: 24 (over z_hi, x, core).
Axes of the slice: x: 4, y: 8, z: 12 (z_hi: 3, z_lo: 4; z = z_hi * 4 + z_lo), core: 2. Of those that a mesh axis runs over, the one named last changes fastest.
Arguments:
- features: bfloat16 [98304, 128], P(('wide', 'rep')), may hold values from -6 to 6
- weight: bfloat16 [128, 256], replicated, may hold values from -0.5 to 0.5
- cotangent: bfloat16 [98304, 256], P(('wide', 'rep')), may hold values from -6 to 6
- tile_values: bfloat16 [32, 24, 32, 4, 128, 128], P('wide', 'rep'), may hold values from -0.09375 to 0.09375
- tile_rows: int32 [32, 24, 32, 4], P('wide', 'rep'), may hold values from 0 to 23, as said below
- tile_counts: int32 [32, 24, 32], P('wide', 'rep'), may hold values from 0 to 4, as said below
Outputs:
- output: bfloat16 [98304, 256], P(('wide', 'rep'))
- weight_grad: float32 [128, 256], replicated
- feature_grad: bfloat16 [98304, 128], P(('wide', 'rep'))
Inputs may be any that keep to these rules, and one draw needn't show every extreme that they name: `tile_rows`: the 4 row tiles of each list are distinct. `tile_counts`: in some row block every list is full.
All inputs are finite; a program needn't handle non-finite values.
Results may differ from a plain program's by a relative error of at most 0.0065.
Values may be sent and summed in bfloat16 or wider, within the bound.
A program may use at most 32 MiB of HBM per device.

v0:
```python
import math

import jax
import jax.numpy as jnp
from jax import lax
from jax.sharding import PartitionSpec as P


def from_behind(value, axis, steps):
    count = lax.axis_size(axis)
    pairs = [(source, (source + steps) % count) for source in range(count)]
    return lax.ppermute(value, axis, pairs)


def silu_slope(hidden):
    sig = jax.nn.sigmoid(hidden)
    return sig * (1.0 + hidden * (1.0 - sig))


def shards(features, weight, cotangent, tile_values, tile_rows, tile_counts):
    tile_block_list = tile_values[0, 0]
    row_tiles = tile_rows[0, 0]
    live_counts = tile_counts[0, 0]
    wide_count = lax.axis_size("wide")
    rep_count = lax.axis_size("rep")
    slot_count = tile_block_list.shape[1]
    tile_size = tile_block_list.shape[2]
    feat_width = features.shape[1]
    position = lax.axis_index("wide")
    live_mask = lax.broadcasted_iota(jnp.int32, (wide_count, slot_count), 1) < live_counts[:, None]

    def accumulate(total, source, shard_rows):
        tile_group = lax.dynamic_index_in_dim(tile_block_list, source, 0, keepdims=False)
        summands = jnp.einsum(
            "kab,bf->kaf", tile_group, shard_rows, preferred_element_type=jnp.float32
        )
        targets = lax.dynamic_index_in_dim(row_tiles, source, 0, keepdims=False)
        alive = lax.dynamic_index_in_dim(live_mask, source, 0, keepdims=False)
        summands = jnp.where(alive[:, None, None], summands, jnp.float32(0.0))
        return total.at[targets].add(summands)

    def advance(carry, step_index):
        shard_rows, total = carry
        moved = from_behind(shard_rows, "wide", 1)
        source = (position - step_index) % wide_count
        return ((moved, accumulate(total, source, moved)), None)

    start_total = jnp.zeros((rep_count, tile_size, feat_width), jnp.float32)
    start_total = accumulate(start_total, position, features)
    (_, partial_sum), _ = lax.scan(
        advance, (features, start_total), jnp.arange(1, wide_count, dtype=jnp.int32)
    )
    partial_sum = partial_sum.reshape(rep_count * tile_size, feat_width)
    own_rows = lax.psum_scatter(partial_sum, "rep", scatter_dimension=0, tiled=True)
    aggregated = own_rows.astype(jnp.bfloat16)
    hidden = jnp.dot(aggregated, weight, preferred_element_type=jnp.float32)
    output = jax.nn.silu(hidden).astype(jnp.bfloat16)
    grad_hidden = (cotangent.astype(jnp.float32) * silu_slope(hidden)).astype(jnp.bfloat16)
    weight_term = jnp.einsum(
        "nf,nh->fh", aggregated, grad_hidden, preferred_element_type=jnp.float32
    )
    grad_own = jnp.einsum(
        "nh,fh->nf", grad_hidden, weight, preferred_element_type=jnp.float32
    ).astype(jnp.bfloat16)
    grad_whole = lax.all_gather(grad_own, "rep", axis=0, tiled=True)
    grad_tiles = grad_whole.reshape(rep_count, tile_size, feat_width)
    picked = jnp.take(grad_tiles, row_tiles, axis=0)
    chosen_entries = jnp.where(live_mask[:, :, None, None], picked, jnp.zeros_like(picked))
    summands = jnp.einsum(
        "lhjz,lhjq->lzq", tile_block_list, chosen_entries, preferred_element_type=jnp.float32
    )
    feature_grad = lax.psum_scatter(
        summands.reshape(tile_size * lax.axis_size("wide"), feat_width),
        "wide",
        scatter_dimension=0,
        tiled=True,
    ).astype(jnp.bfloat16)
    gradient_scale = 1.0 / math.sqrt(wide_count * rep_count * tile_size)
    weight_grad = lax.psum(weight_term, ("wide", "rep")) * gradient_scale
    return (output, weight_grad, feature_grad)


def solution(mesh):
    in_specs = (
        P(("wide", "rep"), None),
        P(),
        P(("wide", "rep"), None),
        P("wide", "rep", None, None, None, None),
        P("wide", "rep", None, None),
        P("wide", "rep", None),
    )
    out_specs = (P(("wide", "rep"), None), P(), P(("wide", "rep"), None))
    return jax.shard_map(shards, mesh=mesh, in_specs=in_specs, out_specs=out_specs, check_vma=False)
```

profile of v0, /device:TPU:6, one launch (start us, length us, event | category | flops | bytes accessed | tf_op | source)
XLA Modules:
  0.0 1137.4 jit_solution(16461475871394044062)
XLA Ops:
  12.4 362.0 %while.14 = (s32[]{:T(128)}, bf16[128,128]{1,0:T(8,128)(2,1)S(1)}, f32[24,128,128]{2,1,0:T(8,128)S(1)}, s32[31]{0:T(128)S(1)}, s32[]{:T(128)}, /*index=5*/s32[32...) while((s32[]{:T(128)}, bf16[128,128]{1,0:T(8,128)(2,1)S(1)}, ...), condition=%wide.region_3.4_spmd, body=%wide.region_1.3_spmd.sunk | while | flops 16908316 | bytes 1409420 | solution.py:50
  17.3 7.9 collective-permute-done
  30.3 6.5 collective-permute-done
  41.9 6.5 collective-permute-done
  53.5 6.5 collective-permute-done
  65.1 6.5 collective-permute-done
  76.6 6.5 collective-permute-done
  88.2 6.5 collective-permute-done
  99.8 6.5 collective-permute-done
  111.4 6.5 collective-permute-done
  146.1 6.5 collective-permute-done
  180.8 6.5 collective-permute-done
  204.0 6.5 collective-permute-done
  238.7 6.5 collective-permute-done
  273.5 6.5 collective-permute-done
  296.6 6.5 collective-permute-done
  308.2 6.5 collective-permute-done
  331.4 6.5 collective-permute-done
  366.1 6.5 collective-permute-done
  376.0 128.2 %reduce-scatter.3.cloned.1.call-done = f32[128,128]{1,0:T(8,128)} async-done(((f32[3072,128]{1,0:T(8,128)}), f32[128,128]{1,0:T(8,128)}) %reduce-scatter.3.cloned.1.call-update) | async-done | bytes 65552 | tf_op jit(solution)/shard_map/reduce_scatter | solution.py:54
  507.8 37.4 %all_gather.3 = bf16[3072,128]{1,0:T(8,128)(2,1)S(1)} all-gather(bf16[128,128]{1,0:T(8,128)(2,1)S(1)} %convolution_convert_fusion), channel_id=1, replica_groups=mesh['wide'=32,'rep'=24] {'rep'}, dimensions={0}, use_global_device_ids=true | all-gather | bytes 819200 | tf_op jit(solution)/shard_map/all_gather | solution.py:65
  548.2 6.6 fusion.6
  554.8 410.2 %all-reduce.2.cloned.1.call-done = f32[128,256]{1,0:T(8,128)} async-done(((f32[128,256]{1,0:T(8,128)}), f32[128,256]{1,0:T(8,128)}) %all-reduce.2.cloned.1.call-update) | async-done | bytes 131088 | tf_op jit(solution)/shard_map/psum | solution.py:79
  966.6 162.8 %reduce-scatter.5.cloned.1.call-done = f32[128,128]{1,0:T(8,128)} async-done(((f32[4096,128]{1,0:T(8,128)}), f32[128,128]{1,0:T(8,128)}) %reduce-scatter.5.cloned.1.call-update) | async-done | bytes 65552 | tf_op jit(solution)/shard_map/reduce_scatter | solution.py:72
  (266 shorter events, 237.5 us)
Async XLA Ops:
  7.2 497.0 %reduce-scatter.3.cloned.1.call-start = ((), (), s32[]{:S(2)}) async-start(), calls=%async_computation.2 | async-start | bytes 1638400 | tf_op jit(solution)/shard_map/reduce_scatter | solution.py:54
  12.4 12.8 %collective-permute-start = (bf16[128,128]{1,0:T(8,128)(2,1)S(1)}, bf16[128,128]{1,0:T(8,128)(2,1)S(1)}, u32[]{:S(2)}, u32[]{:S(2)}) collective-permute-start(bf16[128,128]{1,0:T(8,128)(2,1)S(1)} %get-tuple-element.202), channel_id=1, source_target_pairs={{0,24},{24,48},{48,72},{72,96},{96,120},{120,144},{144,168},{168,1... | collective-permute-start | bytes 98312 | tf_op jit(solution)/shard_map/while/body/eval_jaxpr/ppermute | solution.py:12
  27.1 9.7 collective-permute-start
  38.7 9.7 collective-permute-start
  50.2 9.7 collective-permute-start
  61.8 9.7 collective-permute-start
  73.4 9.7 collective-permute-start
  85.0 9.7 collective-permute-start
  96.6 9.7 collective-permute-start
  108.1 9.7 collective-permute-start
  119.7 9.7 collective-permute-start
  131.3 9.7 collective-permute-start
  142.9 9.7 collective-permute-start
  177.6 9.7 collective-permute-start
  200.8 9.7 collective-permute-start
  212.3 9.7 collective-permute-start
  235.5 9.7 collective-permute-start
  270.2 9.7 collective-permute-start
  293.4 9.7 collective-permute-start
  305.0 9.7 collective-permute-start
  328.1 9.7 collective-permute-start
  362.9 9.7 collective-permute-start
  375.6 589.4 %all-reduce.2.cloned.1.call-start = ((), (), s32[]{:S(2)}) async-start(), calls=%async_computation.3 | async-start | bytes 262144 | tf_op jit(solution)/shard_map/psum | solution.py:79
  507.8 621.6 %reduce-scatter.5.cloned.1.call-start = ((), (), s32[]{:S(2)}) async-start(), calls=%async_computation.4 | async-start | bytes 2162688 | tf_op jit(solution)/shard_map/reduce_scatter | solution.py:72
  (14 other events, 1450.5 us)
Sparse Core Ops, SparseCore 0:
  375.7 128.4 reduce-scatter.2
  511.1 453.9 all-reduce.1
  968.1 161.2 reduce-scatter.4
where the time goes:
time: 1140 us
  waiting for transfers between devices  904 us (79%)
  starting transfers between devices  61.3 us (5%)
  matrix products  44.3 us (4%)
  blocking collectives  37.4 us (3%)
  other arithmetic  28.3 us (2%)
  local copies, waits for them, and re-layouts  25.8 us (2%)
  loops' own time  22.7 us (2%)
  between operations  13.8 us (1%)
    psum x1, waiting for transfers between devices, shards(): weight_grad = lax.psum(weight_term, ('wide', 'rep')) * gradient_scale  410 us
    ppermute x31, waiting for transfers between devices, from_behind(): return lax.ppermute(value, axis, pairs)  203 us
    reduce_scatter x1, waiting for transfers between devices, shards(): lax.psum_scatter(summands.reshape(tile_size * lax.axis_size('wide'), feat...  163 us
    reduce_scatter x1, waiting for transfers between devices, shards(): lax.psum_scatter(partial_sum, 'rep', scatter_dimension=0, tiled=True)  128 us
    ppermute x31, starting transfers between devices, from_behind(): return lax.ppermute(value, axis, pairs)  61.2 us
    all_gather x1, blocking collectives, shards(): grad_whole = lax.all_gather(grad_own, 'rep', axis=0, tiled=True)  37.4 us
    dot_general x32, matrix products, accumulate(): jnp.einsum('kab,bf->kaf', tile_group, shard_rows, preferred_element_type=...  34.2 us
    scatter-add x32, other arithmetic, accumulate(): return total.at[targets].add(summands)  24.1 us
  transfers between devices with their start and end apart: 34, of which 34 were waited for; matrix products, arithmetic and copies ran while one was open for 3% of the time, Pallas kernels for 0%

commit v1 on v0

v1 whole, which is shorter than its diff:
```python
import math

import jax
import jax.numpy as jnp
from jax import lax
from jax.experimental import pallas as pl
from jax.experimental.pallas import tpu as pltpu
from jax.sharding import PartitionSpec as P

MESH = pl.DeviceIdType.MESH
T = 128
NY, NZL, NZH, NX = 8, 4, 3, 4
N_WIDE, N_REP, KT = 32, 24, 4
BF = jnp.bfloat16
F32 = jnp.float32
X_ORDER = (2, 1, 3)


def place():
    wide = lax.axis_index("wide")
    rep = lax.axis_index("rep")
    y, zl = lax.rem(wide, NY), wide // NY
    core, x, zh = lax.rem(rep, 2), lax.rem(rep // 2, NX), rep // (2 * NX)
    return x, y, zl, zh, core


def kernel(
    feat, weight, cot, tiles_hbm, table,
    out_ref, wgrad_ref, fgrad_ref,
    tiles, xs, tot, sib_s, sib_r, x_s, x_r, z_s, z_r, g, y_s, y_r, f_s, f_r,
    w_t, w_r1, w_a, w_r2, w_c, w_d, w_e, w_o,
    tile_sem, ag_zs, ag_ys, ag_r, sib_ss, sib_rs, x_ss, x_rs, z_ss, z_rs,
    g_ss, g_rs, y_ss, y_rs, f_ss, f_rs, w_ss, w_rs,
):
    x, y, zl, zh, core = place()

    def dev(x=x, y=y, zl=zl, zh=zh, core=core):
        return (zl * NY + y, zh * (2 * NX) + x * 2 + core)

    def up(v, by, n):
        return lax.rem(v + by, n)

    sibling = dev(core=1 - core)

    def send(src, dst, ss, rs, to):
        pltpu.make_async_remote_copy(
            src_ref=src, dst_ref=dst, send_sem=ss, recv_sem=rs,
            device_id=to, device_id_type=MESH,
        ).start()

    def wait_recv(dst, rs):
        pltpu.make_async_remote_copy(
            src_ref=dst, dst_ref=dst, send_sem=rs, recv_sem=rs,
            device_id=sibling, device_id_type=MESH,
        ).wait_recv()

    def wait_send(src, ss):
        pltpu.make_async_remote_copy(
            src_ref=src, dst_ref=src, send_sem=ss, recv_sem=ss,
            device_id=sibling, device_id_type=MESH,
        ).wait_send()

    load = pltpu.make_async_copy(tiles_hbm, tiles, tile_sem)
    load.start()

    barrier = pltpu.get_barrier_semaphore()
    partners = [sibling]
    partners += [dev(x=up(x, d, NX)) for d in range(1, NX)]
    partners += [dev(y=up(y, d, NY)) for d in range(1, NY)]
    partners += [dev(zl=up(zl, d, NZL)) for d in range(1, NZL)]
    partners += [dev(zh=up(zh, d, NZH)) for d in range(1, NZH)]
    for partner in partners:
        pl.semaphore_signal(barrier, inc=1, device_id=partner, device_id_type=MESH)

    own = zl * NY + y
    xs[own] = feat[...]
    tot[N_WIDE * KT] = jnp.zeros((T, T), F32)
    g[N_REP] = jnp.zeros((T, T), BF)
    pl.semaphore_wait(barrier, len(partners))

    y_next, y_prev = dev(y=up(y, 1, NY)), dev(y=up(y, NY - 1, NY))

    def block(d, dy):
        return up(zl, d, NZL) * NY + up(y, dy, NY)

    def forward_up(h, d, c):
        send(xs.at[c], xs.at[c], ag_ys.at[0, h, d], ag_r.at[c], y_next)

    def forward_down(h, d, c):
        send(xs.at[c], xs.at[c], ag_ys.at[1, h, d], ag_r.at[c], y_prev)

    for d in range(1, NZL):
        send(xs.at[own], xs.at[own], ag_zs.at[d - 1], ag_r.at[own], dev(zl=up(zl, d, NZL)))
    forward_up(0, 0, own)
    forward_down(0, 0, own)
    load.wait()

    def process(rank, c):
        product = jnp.dot(
            tiles[c].reshape(KT * T, T), xs[c], preferred_element_type=F32
        )
        for k in range(KT):
            before = table[c * KT + k]
            tot[rank * KT + k] = product[k * T:(k + 1) * T] + tot[before]

    process(0, own)

    def z_step(d, carry):
        c = block(d, 0)
        wait_recv(xs.at[c], ag_r.at[c])
        forward_up(0, d, c)
        forward_down(0, d, c)
        process(d, c)
        return carry

    lax.fori_loop(1, NZL, z_step, 0)

    def y_step(step, carry):
        h, d = step // NZL + 1, lax.rem(step, NZL)
        c = block(d, NY - h)
        wait_recv(xs.at[c], ag_r.at[c])

        @pl.when((h < 3) | (d < 2))
        def _():
            forward_up(h, d, c)

        e = block(d, h)
        wait_recv(xs.at[e], ag_r.at[e])

        @pl.when((h < 3) | (d >= 2))
        def _():
            forward_down(h, d, e)

        process(NZL + 2 * step, c)
        process(NZL + 2 * step + 1, e)
        return carry

    lax.fori_loop(0, 3 * NZL, y_step, 0)

    def last_step(d, carry):
        c = block(d, 4)
        wait_recv(xs.at[c], ag_r.at[c])
        process(28 + d, c)
        return carry

    lax.fori_loop(0, NZL, last_step, 0)

    def part(zh_to, x_to, core_to):
        r = zh_to * (2 * NX) + x_to * 2 + core_to
        return tot[table[2 * N_WIDE * KT + r]]

    for n, dx in enumerate(X_ORDER + (0,)):
        for q in range(NZH):
            sib_s[n, q] = part(q, up(x, dx, NX), 1 - core)
        send(sib_s.at[n], sib_r.at[n], sib_ss.at[n], sib_rs.at[n], sibling)
    for n, dx in enumerate(X_ORDER):
        wait_recv(sib_r.at[n], sib_rs.at[n])
        for q in range(NZH):
            x_s[n, q] = (part(q, up(x, dx, NX), core) + sib_r[n, q]).astype(BF)
        send(x_s.at[n], x_r.at[n], x_ss.at[n], x_rs.at[n], dev(x=up(x, dx, NX)))
    wait_recv(sib_r.at[3], sib_rs.at[3])
    for n in range(3):
        wait_recv(x_r.at[n], x_rs.at[n])

    def column_sum(q):
        value = part(q, x, core) + sib_r[3, q]
        for n in range(3):
            value = value + x_r[n, q].astype(F32)
        return value

    for n in range(2):
        q = up(zh, n + 1, NZH)
        z_s[n] = column_sum(q).astype(BF)
        send(z_s.at[n], z_r.at[n], z_ss.at[n], z_rs.at[n], dev(zh=q))
    total = column_sum(zh)
    for n in range(2):
        wait_recv(z_r.at[n], z_rs.at[n])
        total = total + z_r[n].astype(F32)

    agg = total.astype(BF)
    hidden = jnp.dot(agg, weight[...], preferred_element_type=F32)
    sig = jax.nn.sigmoid(hidden)
    grad_hidden = (cot[...].astype(F32) * (sig * (1.0 + hidden * (1.0 - sig)))).astype(BF)
    grad_t = lax.dot_general(
        weight[...], grad_hidden, (((1,), (1,)), ((), ())), preferred_element_type=F32
    )
    mine = zh * (2 * NX) + x * 2 + core
    g[mine] = grad_t.astype(BF)

    def g_send(n, r, to):
        send(g.at[r], g.at[r], g_ss.at[n], g_rs.at[r], to)

    for n in range(2):
        g_send(n, mine, dev(zh=up(zh, n + 1, NZH)))
    for n, dx in enumerate(X_ORDER):
        g_send(2 + n, mine, dev(x=up(x, dx, NX)))
    g_send(5, mine, sibling)

    out_ref[...] = (hidden * sig).astype(BF)
    w_t[...] = lax.dot_general(
        agg, grad_hidden, (((0,), (0,)), ((), ())), preferred_element_type=F32
    )
    half = T // 2
    chunk = half // NX
    mine_half = pl.ds(pl.multiple_of(core * half, half), half)
    other_half = pl.ds(pl.multiple_of((1 - core) * half, half), half)
    send(w_t.at[other_half], w_r1, w_ss.at[0], w_rs.at[0], sibling)

    for n in range(2):
        r = up(zh, 2 - n, NZH) * (2 * NX) + x * 2 + core
        wait_recv(g.at[r], g_rs.at[r])
        for m, dx in enumerate(X_ORDER):
            g_send(6 + 4 * n + m, r, dev(x=up(x, dx, NX)))
        g_send(6 + 4 * n + 3, r, sibling)

    wait_recv(w_r1, w_rs.at[0])
    w_a[...] = w_t[mine_half] + w_r1[...]

    def chunk_of(v):
        return pl.ds(pl.multiple_of(v * chunk, chunk), chunk)

    for n, dx in enumerate(X_ORDER):
        to = up(x, dx, NX)
        send(w_a.at[chunk_of(to)], w_r2.at[n], w_ss.at[1 + n], w_rs.at[1 + n], dev(x=to))

    for q in range(NZH):
        for n, dx in enumerate(X_ORDER):
            r = up(zh, NZH - q, NZH) * (2 * NX) + up(x, NX - dx, NX) * 2 + core
            wait_recv(g.at[r], g_rs.at[r])
            g_send(14 + 3 * q + n, r, sibling)

    w_sum = w_a[chunk_of(x)]
    for n in range(3):
        wait_recv(w_r2.at[n], w_rs.at[1 + n])
        w_sum = w_sum + w_r2[n]
    w_c[y] = w_sum
    for n in range(1, NY):
        send(w_c.at[y], w_c.at[y], w_ss.at[3 + n], w_rs.at[4 + y], dev(y=up(y, n, NY)))

    def sib_wait(n, carry):
        r = n * 2 + 1 - core
        wait_recv(g.at[r], g_rs.at[r])
        return carry

    lax.fori_loop(0, N_REP // 2, sib_wait, 0)

    def term(c):
        left = jnp.concatenate(
            [g[table[N_WIDE * KT + c * KT + k]] for k in range(KT)], axis=1
        )
        return jnp.dot(left, tiles[c].reshape(KT * T, T), preferred_element_type=F32)

    def y_send(side, h, d, value):
        y_s[side, h - 1, d] = value.astype(BF)
        send(
            y_s.at[side, h - 1, d], y_r.at[side, h - 1, d],
            y_ss.at[side, h - 1, d], y_rs.at[side, h - 1, d],
            y_next if side == 0 else y_prev,
        )

    def arrived(side, h, d):
        wait_recv(y_r.at[side, h, d], y_rs.at[side, h, d])
        return y_r[side, h, d].astype(F32)

    def first(d, carry):
        y_send(0, 4, d, term(block(d, 4)))
        y_send(1, 4, d + 2, term(block(d + 2, 4)))
        return carry

    lax.fori_loop(0, 2, first, 0)

    def second(d, carry):
        y_send(0, 3, d + 2, term(block(d + 2, 3)))
        y_send(1, 3, d, term(block(d, NY - 3)))
        return carry

    lax.fori_loop(0, 2, second, 0)

    def third(d, carry):
        own_up = term(block(d, 3))
        own_down = term(block(d + 2, NY - 3))
        y_send(0, 3, d, own_up + arrived(0, 3, d))
        y_send(1, 3, d + 2, own_down + arrived(1, 3, d + 2))
        return carry

    lax.fori_loop(0, 2, third, 0)

    def ring(h):
        def body(d, carry):
            own_up = term(block(d, h))
            own_down = term(block(d, NY - h))
            y_send(0, h, d, own_up + arrived(0, h, d))
            y_send(1, h, d, own_down + arrived(1, h, d))
            return carry

        lax.fori_loop(0, NZL, body, 0)

    def spread_sum(buf, base, me, n):
        def wait_one(i, carry):
            @pl.when(i != me)
            def _():
                wait_recv(buf.at[i], w_rs.at[base + i])
            return carry

        lax.fori_loop(0, n, wait_one, 0)
        value = buf[0]
        for i in range(1, n):
            value = value + buf[i]
        return value

    w_d[zl] = spread_sum(w_c, 4, y, NY)
    for n in range(1, NZL):
        send(w_d.at[zl], w_d.at[zl], w_ss.at[10 + n], w_rs.at[12 + zl], dev(zl=up(zl, n, NZL)))

    ring(2)

    w_e[zh] = spread_sum(w_d, 12, zl, NZL)
    for n in range(1, NZH):
        send(w_e.at[zh], w_e.at[zh], w_ss.at[13 + n], w_rs.at[16 + zh], dev(zh=up(zh, n, NZH)))

    ring(1)

    w_own = spread_sum(w_e, 16, zh, NZH) * (1.0 / math.sqrt(N_WIDE * N_REP * T))
    w_o[core, x] = w_own
    for n in range(1, NX):
        send(w_o.at[core, x], w_o.at[core, x], w_ss.at[15 + n], w_rs.at[19 + x], dev(x=up(x, n, NX)))

    def last(d, carry):
        value = term(block(d, 0)) + arrived(0, 0, d)
        f_s[d - 1] = (value + arrived(1, 0, d)).astype(BF)
        send(f_s.at[d - 1], f_r.at[d - 1], f_ss.at[d - 1], f_rs.at[d - 1], dev(zl=up(zl, d, NZL)))
        return carry

    lax.fori_loop(1, NZL, last, 0)
    value = term(block(0, 0)) + arrived(0, 0, 0) + arrived(1, 0, 0)

    def gathered(i, carry):
        @pl.when(i != x)
        def _():
            wait_recv(w_o.at[core, i], w_rs.at[19 + i])
        return carry

    lax.fori_loop(0, NX, gathered, 0)
    send(w_o.at[core], w_o.at[core], w_ss.at[19], w_rs.at[23], sibling)

    for n in range(3):
        wait_recv(f_r.at[n], f_rs.at[n])
        value = value + f_r[n].astype(F32)
    fgrad_ref[...] = value.T.astype(BF)
    wait_recv(w_o.at[1 - core], w_rs.at[23])
    wgrad_ref[...] = w_o[...].reshape(T, 2 * T)

    for n in range(3):
        wait_send(xs.at[0], ag_zs.at[n])
    for n in range(3):
        wait_send(x_s.at[n], x_ss.at[n])
        wait_send(f_s.at[n], f_ss.at[n])
    for n in range(4):
        wait_send(sib_s.at[n], sib_ss.at[n])
    for n in range(2):
        wait_send(z_s.at[n], z_ss.at[n])

    def drain(step, carry):
        h, d = step // NZL, lax.rem(step, NZL)

        @pl.when((h < 3) | (d < 2))
        def _():
            wait_send(xs.at[0], ag_ys.at[0, h, d])
            wait_send(y_s.at[0, h, d], y_ss.at[0, h, d])

        @pl.when((h < 3) | (d >= 2))
        def _():
            wait_send(xs.at[0], ag_ys.at[1, h, d])
            wait_send(y_s.at[1, h, d], y_ss.at[1, h, d])

        return carry

    lax.fori_loop(0, 4 * NZL, drain, 0)

    def drain_g(n, carry):
        wait_send(g.at[0], g_ss.at[n])
        return carry

    lax.fori_loop(0, 23, drain_g, 0)
    wait_send(w_r1, w_ss.at[0])

    def drain_w(n, carry):
        wait_send(w_r2.at[0], w_ss.at[n])
        return carry

    lax.fori_loop(1, 19, drain_w, 0)
    wait_send(w_o.at[core], w_ss.at[19])


def make_table(rows, counts):
    x, y, zl, zh, core = place()
    c = jnp.arange(N_WIDE, dtype=jnp.int32)
    d = (c // NY - zl) % NZL
    dy = (c % NY - y) % NY
    h = jnp.where(dy > 4, NY - dy, dy)
    rank = jnp.where(
        h == 0, d,
        jnp.where(h == 4, 28 + d, NZL + 8 * (h - 1) + 2 * d + jnp.where(dy > 4, 0, 1)),
    )
    slot = jnp.arange(KT, dtype=jnp.int32)
    live = slot[None, :] < counts[:, None]
    code = jnp.where(live, rows, -1).reshape(-1)
    key = (rank[:, None] * KT + slot[None, :]).reshape(-1)
    step = jnp.broadcast_to(rank[:, None], (N_WIDE, KT)).reshape(-1)
    match = (code[:, None] == code[None, :]) & (step[None, :] < step[:, None]) & (code[None, :] >= 0)
    before = jnp.max(jnp.where(match, key[None, :], -1), axis=1)
    before = jnp.where(before < 0, N_WIDE * KT, before)
    owner = jnp.arange(N_REP, dtype=jnp.int32)
    final = jnp.max(jnp.where(code[None, :] == owner[:, None], key[None, :], -1), axis=1)
    final = jnp.where(final < 0, N_WIDE * KT, final)
    chosen = jnp.where(code < 0, N_REP, code)
    return jnp.concatenate([before, chosen, final])


def shards(features, weight, cotangent, tile_values, tile_rows, tile_counts):
    table = make_table(tile_rows[0, 0], tile_counts[0, 0])
    vmem = pl.BlockSpec(memory_space=pltpu.VMEM)
    dma = pltpu.SemaphoreType.DMA
    return pl.pallas_call(
        kernel,
        out_shape=(
            jax.ShapeDtypeStruct((T, 2 * T), BF),
            jax.ShapeDtypeStruct((T, 2 * T), F32),
            jax.ShapeDtypeStruct((T, T), BF),
        ),
        in_specs=[
            vmem, vmem, vmem,
            pl.BlockSpec(memory_space=pl.ANY),
            pl.BlockSpec(memory_space=pltpu.SMEM),
        ],
        out_specs=(vmem, vmem, vmem),
        scratch_shapes=[
            pltpu.VMEM((N_WIDE, KT, T, T), BF),
            pltpu.VMEM((N_WIDE, T, T), BF),
            pltpu.VMEM((N_WIDE * KT + 1, T, T), F32),
            pltpu.VMEM((4, NZH, T, T), F32),
            pltpu.VMEM((4, NZH, T, T), F32),
            pltpu.VMEM((3, NZH, T, T), BF),
            pltpu.VMEM((3, NZH, T, T), BF),
            pltpu.VMEM((2, T, T), BF),
            pltpu.VMEM((2, T, T), BF),
            pltpu.VMEM((N_REP + 1, T, T), BF),
            pltpu.VMEM((2, 4, NZL, T, T), BF),
            pltpu.VMEM((2, 4, NZL, T, T), BF),
            pltpu.VMEM((3, T, T), BF),
            pltpu.VMEM((3, T, T), BF),
            pltpu.VMEM((T, 2 * T), F32),
            pltpu.VMEM((T // 2, 2 * T), F32),
            pltpu.VMEM((T // 2, 2 * T), F32),
            pltpu.VMEM((3, T // 8, 2 * T), F32),
            pltpu.VMEM((NY, T // 8, 2 * T), F32),
            pltpu.VMEM((NZL, T // 8, 2 * T), F32),
            pltpu.VMEM((NZH, T // 8, 2 * T), F32),
            pltpu.VMEM((2, NX, T // 8, 2 * T), F32),
            dma, dma((3,)), dma((2, 4, NZL)), dma((N_WIDE,)),
            dma((4,)), dma((4,)), dma((3,)), dma((3,)), dma((2,)), dma((2,)),
            dma((23,)), dma((N_REP,)), dma((2, 4, NZL)), dma((2, 4, NZL)),
            dma((3,)), dma((3,)), dma((20,)), dma((24,)),
        ],
        compiler_params=pltpu.CompilerParams(
            collective_id=0, has_side_effects=True, vmem_limit_bytes=48 * 1024 * 1024
        ),
        name="graph_layer",
    )(
        features, weight, cotangent,
        tile_values.reshape(N_WIDE, KT, T, T), table,
    )


def solution(mesh):
    in_specs = (
        P(("wide", "rep"), None),
        P(),
        P(("wide", "rep"), None),
        P("wide", "rep", None, None, None, None),
        P("wide", "rep", None, None),
        P("wide", "rep", None),
    )
    out_specs = (P(("wide", "rep"), None), P(), P(("wide", "rep"), None))
    return jax.shard_map(shards, mesh=mesh, in_specs=in_specs, out_specs=out_specs, check_vma=False)
```

time: 1140 us -> 96.2 us (0.08)
  the two profiles are of different devices: /device:TPU:6 before, /device:TPU:1 now
where the time goes in v1:
time: 96.2 us; the launch traced here: 95.9 us
  Pallas kernels  86.2 us (90%)
  local copies, waits for them, and re-layouts  7.79 us (8%)
  other arithmetic  1.15 us (1%)
    pallas_call x1, Pallas kernels, shards(): pl.pallas_call(kernel, out_shape=(jax.ShapeDtypeStruct((T, 2 * T), BF), j...  86.2 us
    unnamed x12, local copies, waits for them, and re-layouts  7.29 us

profile of v1, /device:TPU:1, one launch (start us, length us, event | category | flops | bytes accessed | tf_op | source)
XLA Modules:
  0.0 95.9 jit_solution(14596144050985176944)
XLA Ops:
  0.7 0.7 iota_compare_fusion
  1.4 0.1 lt.75
  1.5 0.1 iota_add_fusion
  1.6 0.1 add.123
  1.7 0.1 broadcast_in_dim.54
  1.8 0.1 lt.79
  1.9 0.8 copy.11
  2.6 0.1 squeeze.3
  2.8 0.2 select_reduce_fusion
  3.0 0.1 select_reduce_fusion.1
  3.1 0.0 copy-start
  3.1 2.2 %copy-done = bf16[1,1,32,4,128,128]{5,4,3,2,1,0:T(8,128)(2,1)S(1)} copy-done((bf16[1,1,32,4,128,128]{5,4,3,2,1,0:T(8,128)(2,1)S(1)}, bf16[1,1,32,4,128,128]{5,4,3,2,1,0:T(8,128)(2,1)}, u32[]{:S(2)}) %copy-start) | copy-done | bytes 4194328
  5.3 0.0 copy-start.1
  5.3 0.8 copy-done.1
  6.1 0.0 copy-start.2
  6.1 0.8 copy-done.2
  7.0 0.0 copy-start.3
  7.0 0.8 copy-done.3
  7.7 86.2 %graph_layer.1 = (bf16[128,256]{1,0:T(8,128)(2,1)S(1)}, f32[128,256]{1,0:T(8,128)S(1)}, bf16[128,128]{1,0:T(8,128)(2,1)S(1)}) custom-call(bf16[128,128]{1,0:T(8,128)(2,1)S(1)} %copy-done.3, bf16[128,256]{1,0:T(8,128)(2,1)S(1)} %copy-done.1, bf16[128,256]{1,0:T(8,128)(2,1)S(1)} %copy-done.2, bf16[32,4,128,128]{3,2,1,0:T(8,128)(2,1)S(1)} %bitcast.4, ...), custom_call_target="tpu_custom_call" | custom-call | tf_op jit(solution)/shard_map/graph_layer/pallas_call | solution.py:424
  94.0 0.6 copy.15
  94.6 0.7 copy.16
  95.3 0.6 copy.17
  (5 shorter events, 0.0 us)
Async XLA Ops:
  3.1 2.2 %copy-start = (bf16[1,1,32,4,128,128]{5,4,3,2,1,0:T(8,128)(2,1)S(1)}, bf16[1,1,32,4,128,128]{5,4,3,2,1,0:T(8,128)(2,1)}, u32[]{:S(2)}) copy-start(bf16[1,1,32,4,128,128]{5,4,3,2,1,0:T(8,128)(2,1)} %param.9) | copy-start | bytes 12582916
  5.3 0.8 copy-start.1
  6.1 0.8 copy-start.2
  7.0 0.8 copy-start.3

commit v2 on v1

v2 whole, which is shorter than its diff:
```python
import math

import jax
import jax.numpy as jnp
from jax import lax
from jax.experimental import pallas as pl
from jax.experimental.pallas import tpu as pltpu
from jax.sharding import PartitionSpec as P

MESH = pl.DeviceIdType.MESH
T = 128
NY, NZL, NZH, NX = 8, 4, 3, 4
N_WIDE, N_REP, KT = 32, 24, 4
BF = jnp.bfloat16
F32 = jnp.float32
X_ORDER = (2, 1, 3)
NEAR, FAR = (-2, 2, -1, 1), (-3, 3, 4)
STEPS = (
    [(0, 0)] + [(0, dy) for dy in NEAR] + [(2, 0), (1, 0), (3, 0)] + [(0, dy) for dy in FAR]
    + [(line, dy) for line in (2, 1, 3) for dy in NEAR]
    + [(line, dy) for line in (1, 2, 3) for dy in FAR]
)


def place():
    wide = lax.axis_index("wide")
    rep = lax.axis_index("rep")
    y, zl = lax.rem(wide, NY), wide // NY
    core, x, zh = lax.rem(rep, 2), lax.rem(rep // 2, NX), rep // (2 * NX)
    return x, y, zl, zh, core


def kernel(
    feat_hbm, weight_hbm, cot_hbm, tiles_hbm, rows_hbm, counts_hbm,
    out_ref, wgrad_ref, fgrad_ref,
    weight, cot, rows, counts, table_v, table, tiles, xs, tot, sib_s, sib_r, x_s, x_r, z_s, z_r, g, y_s, y_r, h_s, h_r, f_s, f_r,
    w_t, w_r1, w_a, w_r2, w_c, w_d, w_e, w_o,
    load_sems, ag_zs, ag_ys, ag_hs, ag_r, sib_ss, sib_rs, x_ss, x_rs, z_ss, z_rs,
    g_ss, g_rs, y_ss, y_rs, h_ss, h_rs, f_ss, f_rs, w_ss, w_rs,
):
    x, y, zl, zh, core = place()

    def dev(x=x, y=y, zl=zl, zh=zh, core=core):
        return (zl * NY + y, zh * (2 * NX) + x * 2 + core)

    def up(v, by, n):
        return lax.rem(v + by, n)

    sibling = dev(core=1 - core)

    def send(src, dst, ss, rs, to):
        pltpu.make_async_remote_copy(
            src_ref=src, dst_ref=dst, send_sem=ss, recv_sem=rs,
            device_id=to, device_id_type=MESH,
        ).start()

    def wait_recv(dst, rs):
        pltpu.make_async_remote_copy(
            src_ref=dst, dst_ref=dst, send_sem=rs, recv_sem=rs,
            device_id=sibling, device_id_type=MESH,
        ).wait_recv()

    def wait_send(src, ss):
        pltpu.make_async_remote_copy(
            src_ref=src, dst_ref=src, send_sem=ss, recv_sem=ss,
            device_id=sibling, device_id_type=MESH,
        ).wait_send()

    own = zl * NY + y
    loads = [
        pltpu.make_async_copy(src, dst, load_sems.at[n])
        for n, (src, dst) in enumerate((
            (feat_hbm, xs.at[own]), (tiles_hbm, tiles), (weight_hbm, weight), (cot_hbm, cot),
            (rows_hbm, rows), (counts_hbm, counts),
        ))
    ]
    for load in loads:
        load.start()

    h_r[1] = jnp.zeros((NY, T, T), BF)
    f_r[1] = jnp.zeros((T, T), BF)
    barrier = pltpu.get_barrier_semaphore()
    partners = [sibling]
    partners += [dev(x=up(x, d, NX)) for d in range(1, NX)]
    partners += [dev(y=up(y, d, NY)) for d in range(1, NY)]
    partners += [dev(zl=up(zl, d, NZL)) for d in range(1, NZL)]
    partners += [dev(zh=up(zh, d, NZH)) for d in range(1, NZH)]
    for partner in partners:
        pl.semaphore_signal(barrier, inc=1, device_id=partner, device_id_type=MESH)

    loads[4].wait()
    loads[5].wait()
    fill_table(rows, counts, table_v)
    table_load = pltpu.make_async_copy(table_v, table, load_sems.at[6])
    table_load.start()
    tot[N_WIDE * KT] = jnp.zeros((T, T), F32)
    g[N_REP] = jnp.zeros((T, T), BF)
    loads[0].wait()
    pl.semaphore_wait(barrier, len(partners))

    y_up, y_down = dev(y=up(y, 1, NY)), dev(y=up(y, NY - 1, NY))
    y_up2, y_down2 = dev(y=up(y, 2, NY)), dev(y=up(y, NY - 2, NY))

    mid = (zl == 1) | (zl == 2)
    even = lax.rem(y, 2) == 0
    lines = (zl, zl + 1 - 2 * lax.rem(zl, 2), up(zl, 2, NZL), NZL - 1 - zl)
    own_line, pair, across, other = range(4)

    def block(line, dy):
        return lines[line] * NY + up(y, (dy + NY) % NY, NY)

    def y_pass(line, n, c, to):
        i = (own_line, across, other).index(line)
        send(xs.at[c], xs.at[c], ag_ys.at[i, n], ag_r.at[c], to)

    def z_pass(dy):
        c = block(own_line, dy)
        send(xs.at[c], xs.at[c], ag_hs.at[0, dy % NY], ag_r.at[c], dev(zl=lines[pair]))

        @pl.when(mid)
        def _():
            send(xs.at[c], xs.at[c], ag_hs.at[1, dy % NY], ag_r.at[c], dev(zl=lines[other]))

    def spread(line):
        c = block(line, 0)
        for n, to in enumerate((y_up2, y_down2, y_up, y_down)):
            y_pass(line, n, c, to)

    def have(line, dy):
        c = block(line, dy)
        wait_recv(xs.at[c], ag_r.at[c])

    def onward(line):
        have(line, -2)
        below = block(line, -2)
        y_pass(line, 4, below, y_up)

        @pl.when(even)
        def _():
            y_pass(line, 6, below, y_up2)

        have(line, 2)
        above = block(line, 2)
        y_pass(line, 5, above, y_down)

        @pl.when(jnp.logical_not(even))
        def _():
            y_pass(line, 6, above, y_down2)

    send(xs.at[own], xs.at[own], ag_zs.at[0], ag_r.at[own], dev(zl=lines[across]))

    @pl.when(jnp.logical_not(mid))
    def _():
        send(xs.at[own], xs.at[own], ag_zs.at[1], ag_r.at[own], dev(zl=lines[other]))

    spread(own_line)
    z_pass(0)
    table_load.wait()
    loads[1].wait()

    def process(rank, c):
        product = jnp.dot(
            tiles[c].reshape(KT * T, T), xs[c], preferred_element_type=F32
        )
        for k in range(KT):
            before = table[k, c]
            tot[rank * KT + k] = product[k * T:(k + 1) * T] + tot[before]

    def work(first, items):
        for n, (line, dy) in enumerate(items):
            process(first + n, block(line, dy))

    process(0, own)
    onward(own_line)
    z_pass(-2)
    z_pass(2)
    have(across, 0)
    spread(across)

    @pl.when(jnp.logical_not(mid))
    def _():
        have(other, 0)
        spread(other)

    have(own_line, -1)
    z_pass(-1)
    have(own_line, 1)
    z_pass(1)
    work(1, STEPS[1:5])
    have(pair, 0)

    @pl.when(mid)
    def _():
        have(other, 0)

    onward(across)

    @pl.when(jnp.logical_not(mid))
    def _():
        onward(other)

    for dy in (-3, 3, 4):
        have(own_line, dy)
        z_pass(dy)
    work(5, STEPS[5:11])
    have(across, -1)
    have(across, 1)
    work(11, STEPS[11:15])
    for dy in (-2, 2, -1, 1):
        have(pair, dy)
    work(15, STEPS[15:19])

    @pl.when(mid)
    def _():
        have(other, -2)
        have(other, 2)

    have(other, -1)
    have(other, 1)
    work(19, STEPS[19:23])
    for first, line in ((23, pair), (26, across), (29, other)):
        for dy in (-3, 3, 4):
            have(line, dy)
        work(first, STEPS[first:first + 3])

    def part(zh_to, x_to, core_to):
        r = zh_to * (2 * NX) + x_to * 2 + core_to
        return tot[table[2 * KT, r]]

    turns = (1, 2, 0)
    for m in turns:
        q = up(zh, m, NZH)
        for n, dx in enumerate(X_ORDER + (0,)):
            sib_s[m, n] = part(q, up(x, dx, NX), 1 - core)
        send(sib_s.at[m], sib_r.at[m], sib_ss.at[m], sib_rs.at[m], sibling)
    for m in turns:
        q = up(zh, m, NZH)
        wait_recv(sib_r.at[m], sib_rs.at[m])
        for n, dx in enumerate(X_ORDER):
            to = up(x, dx, NX)
            x_s[m, n] = (part(q, to, core) + sib_r[m, n]).astype(BF)
            send(x_s.at[m, n], x_r.at[m, n], x_ss.at[m, n], x_rs.at[m, n], dev(x=to))

    def column_sum(m):
        value = part(up(zh, m, NZH), x, core) + sib_r[m, 3]
        for n in range(3):
            wait_recv(x_r.at[m, n], x_rs.at[m, n])
            value = value + x_r[m, n].astype(F32)
        return value

    for n in range(2):
        z_s[n] = column_sum(n + 1).astype(BF)
        send(z_s.at[n], z_r.at[n], z_ss.at[n], z_rs.at[n], dev(zh=up(zh, n + 1, NZH)))
    total = column_sum(0)
    for n in range(2):
        wait_recv(z_r.at[n], z_rs.at[n])
        total = total + z_r[n].astype(F32)

    loads[2].wait()
    loads[3].wait()
    agg = total.astype(BF)
    hidden = jnp.dot(agg, weight[...], preferred_element_type=F32)
    sig = jax.nn.sigmoid(hidden)
    grad_hidden = (cot[...].astype(F32) * (sig * (1.0 + hidden * (1.0 - sig)))).astype(BF)
    grad_t = lax.dot_general(
        weight[...], grad_hidden, (((1,), (1,)), ((), ())), preferred_element_type=F32
    )
    mine = zh * (2 * NX) + x * 2 + core
    g[mine] = grad_t.astype(BF)

    def g_send(n, r, to):
        send(g.at[r], g.at[r], g_ss.at[n], g_rs.at[r], to)

    for n in range(2):
        g_send(n, mine, dev(zh=up(zh, n + 1, NZH)))
    for n, dx in enumerate(X_ORDER):
        g_send(2 + n, mine, dev(x=up(x, dx, NX)))
    g_send(5, mine, sibling)

    out_ref[...] = (hidden * sig).astype(BF)
    w_t[...] = lax.dot_general(
        agg, grad_hidden, (((0,), (0,)), ((), ())), preferred_element_type=F32
    )
    half = T // 2
    chunk = half // NX
    mine_half = pl.ds(pl.multiple_of(core * half, half), half)
    other_half = pl.ds(pl.multiple_of((1 - core) * half, half), half)
    send(w_t.at[other_half], w_r1, w_ss.at[0], w_rs.at[0], sibling)

    for n in range(2):
        r = up(zh, 2 - n, NZH) * (2 * NX) + x * 2 + core
        wait_recv(g.at[r], g_rs.at[r])
        for m, dx in enumerate(X_ORDER):
            g_send(6 + 4 * n + m, r, dev(x=up(x, dx, NX)))
        g_send(6 + 4 * n + 3, r, sibling)

    wait_recv(w_r1, w_rs.at[0])
    w_a[...] = w_t[mine_half] + w_r1[...]

    def chunk_of(v):
        return pl.ds(pl.multiple_of(v * chunk, chunk), chunk)

    for n, dx in enumerate(X_ORDER):
        to = up(x, dx, NX)
        send(w_a.at[chunk_of(to)], w_r2.at[n], w_ss.at[1 + n], w_rs.at[1 + n], dev(x=to))

    for q in range(NZH):
        for n, dx in enumerate(X_ORDER):
            r = up(zh, NZH - q, NZH) * (2 * NX) + up(x, NX - dx, NX) * 2 + core
            wait_recv(g.at[r], g_rs.at[r])
            g_send(14 + 3 * q + n, r, sibling)

    w_sum = w_a[chunk_of(x)]
    for n in range(3):
        wait_recv(w_r2.at[n], w_rs.at[1 + n])
        w_sum = w_sum + w_r2[n]
    w_c[y] = w_sum
    for n in range(1, NY):
        send(w_c.at[y], w_c.at[y], w_ss.at[3 + n], w_rs.at[4 + y], dev(y=up(y, n, NY)))

    def sib_wait(n, carry):
        r = n * 2 + 1 - core
        wait_recv(g.at[r], g_rs.at[r])
        return carry

    lax.fori_loop(0, N_REP // 2, sib_wait, 0)

    def term(c):
        left = jnp.concatenate(
            [g[table[KT + k, c]] for k in range(KT)], axis=1
        )
        return jnp.dot(left, tiles[c].reshape(KT * T, T), preferred_element_type=F32)

    def y_send(line, n, value, to):
        i = (own_line, across, other).index(line)
        y_s[i, n] = value.astype(BF)
        send(y_s.at[i, n], y_r.at[i, n], y_ss.at[i, n], y_rs.at[i, n], to)

    def y_have(line, n):
        i = (own_line, across, other).index(line)
        wait_recv(y_r.at[i, n], y_rs.at[i, n])
        return y_r[i, n].astype(F32)

    def hop(slot, line, dy):
        k = dy % NY
        h_s[slot, k] = term(block(line, dy)).astype(BF)
        send(h_s.at[slot, k], h_r.at[slot, k], h_ss.at[slot, k], h_rs.at[slot, k], dev(zl=lines[line]))

    def value_of(line, dy):
        value = term(block(line, dy))
        if line == own_line:
            k = dy % NY
            wait_recv(h_r.at[0, k], h_rs.at[0, k])
            value = value + h_r[0, k].astype(F32)

            @pl.when(mid)
            def _():
                wait_recv(h_r.at[1, k], h_rs.at[1, k])

            value = value + jnp.where(mid, h_r[1, k].astype(F32), 0.0)
        return value

    def outer_part(line):
        value = value_of(line, 4)

        @pl.when(even)
        def _():
            y_send(line, 0, value, y_up2)

        @pl.when(jnp.logical_not(even))
        def _():
            y_send(line, 0, value, y_down2)

        above, below = value_of(line, 3), value_of(line, -3)
        y_send(line, 1, above, y_up)
        y_send(line, 2, below, y_down)

    def next_part(line):
        above, below = value_of(line, 1), value_of(line, -1)
        y_send(line, 3, above, y_up)
        y_send(line, 4, below, y_down)

    def second_part(line):
        above, below = value_of(line, 2), value_of(line, -2)
        above = above + y_have(line, 1)
        below = below + y_have(line, 2)
        four = y_have(line, 0)
        y_send(line, 5, above + jnp.where(even, four, 0.0), y_up2)
        y_send(line, 6, below + jnp.where(even, 0.0, four), y_down2)

    def whole(line):
        value = value_of(line, 0)
        for n in range(3, 7):
            value = value + y_have(line, n)
        return value

    def z_send(n, line):
        f_s[n] = whole(line).astype(BF)
        send(f_s.at[n], f_r.at[n], f_ss.at[n], f_rs.at[n], dev(zl=lines[line]))

    for dy in FAR:
        hop(0, pair, dy)

    @pl.when(mid)
    def _():
        for dy in FAR:
            hop(1, other, dy)

    outer_part(across)

    @pl.when(jnp.logical_not(mid))
    def _():
        outer_part(other)

    for dy in NEAR + (0,):
        hop(0, pair, dy)

    @pl.when(mid)
    def _():
        for dy in NEAR + (0,):
            hop(1, other, dy)

    outer_part(own_line)

    def spread_sum(buf, base, me, n):
        def wait_one(i, carry):
            @pl.when(i != me)
            def _():
                wait_recv(buf.at[i], w_rs.at[base + i])
            return carry

        lax.fori_loop(0, n, wait_one, 0)
        value = buf[0]
        for i in range(1, n):
            value = value + buf[i]
        return value

    w_d[zl] = spread_sum(w_c, 4, y, NY)
    for n in range(1, NZL):
        send(w_d.at[zl], w_d.at[zl], w_ss.at[10 + n], w_rs.at[12 + zl], dev(zl=up(zl, n, NZL)))

    second_part(across)

    @pl.when(jnp.logical_not(mid))
    def _():
        second_part(other)

    next_part(across)

    @pl.when(jnp.logical_not(mid))
    def _():
        next_part(other)

    next_part(own_line)

    w_e[zh] = spread_sum(w_d, 12, zl, NZL)
    for n in range(1, NZH):
        send(w_e.at[zh], w_e.at[zh], w_ss.at[13 + n], w_rs.at[16 + zh], dev(zh=up(zh, n, NZH)))

    second_part(own_line)
    z_send(0, across)

    @pl.when(jnp.logical_not(mid))
    def _():
        z_send(1, other)

    value = whole(own_line)

    w_own = spread_sum(w_e, 16, zh, NZH) * (1.0 / math.sqrt(N_WIDE * N_REP * T))
    w_o[core, x] = w_own
    for n in range(1, NX):
        send(w_o.at[core, x], w_o.at[core, x], w_ss.at[15 + n], w_rs.at[19 + x], dev(x=up(x, n, NX)))

    def gathered(i, carry):
        @pl.when(i != x)
        def _():
            wait_recv(w_o.at[core, i], w_rs.at[19 + i])
        return carry

    lax.fori_loop(0, NX, gathered, 0)
    send(w_o.at[core], w_o.at[core], w_ss.at[19], w_rs.at[23], sibling)

    wait_recv(f_r.at[0], f_rs.at[0])
    value = value + f_r[0].astype(F32)

    @pl.when(jnp.logical_not(mid))
    def _():
        wait_recv(f_r.at[1], f_rs.at[1])

    value = value + jnp.where(mid, 0.0, f_r[1].astype(F32))
    fgrad_ref[...] = value.T.astype(BF)
    wait_recv(w_o.at[1 - core], w_rs.at[23])
    wgrad_ref[...] = w_o[...].reshape(T, 2 * T)

    def settle(n, carry):
        wait_send(xs.at[0], ag_hs.at[0, n])
        wait_send(h_s.at[0, n], h_ss.at[0, n])

        @pl.when(mid)
        def _():
            wait_send(xs.at[0], ag_hs.at[1, n])
            wait_send(h_s.at[1, n], h_ss.at[1, n])

        return carry

    lax.fori_loop(0, NY, settle, 0)

    def drain(n, carry):
        for i in range(2):
            wait_send(xs.at[0], ag_ys.at[i, n])
            wait_send(y_s.at[i, n], y_ss.at[i, n])

        @pl.when(jnp.logical_not(mid))
        def _():
            wait_send(xs.at[0], ag_ys.at[2, n])
            wait_send(y_s.at[2, n], y_ss.at[2, n])

        return carry

    lax.fori_loop(0, 7, drain, 0)
    wait_send(xs.at[0], ag_zs.at[0])
    wait_send(f_s.at[0], f_ss.at[0])

    @pl.when(jnp.logical_not(mid))
    def _():
        wait_send(xs.at[0], ag_zs.at[1])
        wait_send(f_s.at[1], f_ss.at[1])

    for n in range(2):
        wait_send(z_s.at[n], z_ss.at[n])
    for m in range(NZH):
        wait_send(sib_s.at[m], sib_ss.at[m])
        for n in range(3):
            wait_send(x_s.at[m, n], x_ss.at[m, n])

    def drain_g(n, carry):
        wait_send(g.at[0], g_ss.at[n])
        return carry

    lax.fori_loop(0, 23, drain_g, 0)
    wait_send(w_r1, w_ss.at[0])

    def drain_w(n, carry):
        wait_send(w_r2.at[0], w_ss.at[n])
        return carry

    lax.fori_loop(1, 19, drain_w, 0)
    wait_send(w_o.at[core], w_ss.at[19])


def rank_of(c):
    x, y, zl, zh, core = place()
    v = c // NY
    line = jnp.where(v == zl, 0, jnp.where(v == NZL - 1 - zl, 3, jnp.where(lax.rem(v + zl, 2) == 0, 2, 1)))
    dy = lax.rem(lax.rem(c, NY) - y + NY, NY)
    rank = jnp.zeros_like(c)
    for n, (on, at) in enumerate(STEPS):
        rank = jnp.where((line == on) & (dy == at % NY), n, rank)
    return rank


def fill_table(rows, counts, table_v):
    square = (N_WIDE, N_WIDE)
    lane = lax.broadcasted_iota(jnp.int32, square, 1)
    sub = lax.broadcasted_iota(jnp.int32, square, 0)
    rank_l, rank_s = rank_of(lane), rank_of(sub)
    live = counts[...]
    code = [jnp.where(live > k, rows[k:k + 1, :], -1) for k in range(KT)]
    code_l = [jnp.broadcast_to(v, square) for v in code]
    code_s = [
        jnp.broadcast_to(
            jnp.max(jnp.where(lane == sub, v, -1), axis=1, keepdims=True), square
        )
        for v in code_l
    ]
    none = N_WIDE * KT

    def best(matches):
        keys = [jnp.where(m, rank_s * KT + k, -1) for k, m in enumerate(matches)]
        top = keys[0]
        for key in keys[1:]:
            top = jnp.maximum(top, key)
        top = jnp.max(top, axis=0, keepdims=True)
        return jnp.where(top < 0, none, top)

    for k in range(KT):
        table_v[k:k + 1, 0:N_WIDE] = best(
            [(v == code_l[k]) & (rank_s < rank_l) & (v >= 0) for v in code_s]
        )
        table_v[KT + k:KT + k + 1, 0:N_WIDE] = jnp.where(code[k] < 0, N_REP, code[k])
    table_v[2 * KT:2 * KT + 1, 0:N_WIDE] = best([v == lane for v in code_s])


def shards(features, weight, cotangent, tile_values, tile_rows, tile_counts):
    dma = pltpu.SemaphoreType.DMA
    hbm = pl.BlockSpec(memory_space=pltpu.HBM)
    vmem = pl.BlockSpec(memory_space=pltpu.VMEM)
    shapes = (
        jax.ShapeDtypeStruct((T, 2 * T), BF),
        jax.ShapeDtypeStruct((T, 2 * T), F32),
        jax.ShapeDtypeStruct((T, T), BF),
    )
    return pl.pallas_call(
        kernel,
        out_shape=shapes,
        in_specs=[hbm] * 6,
        out_specs=(vmem, vmem, vmem),
        scratch_shapes=[
            pltpu.VMEM((T, 2 * T), BF),
            pltpu.VMEM((T, 2 * T), BF),
            pltpu.VMEM((KT, N_WIDE), jnp.int32),
            pltpu.VMEM((1, N_WIDE), jnp.int32),
            pltpu.VMEM((16, T), jnp.int32),
            pltpu.SMEM((16, T), jnp.int32),
            pltpu.VMEM((N_WIDE, KT, T, T), BF),
            pltpu.VMEM((N_WIDE, T, T), BF),
            pltpu.VMEM((N_WIDE * KT + 1, T, T), F32),
            pltpu.VMEM((NZH, 4, T, T), F32),
            pltpu.VMEM((NZH, 4, T, T), F32),
            pltpu.VMEM((NZH, 3, T, T), BF),
            pltpu.VMEM((NZH, 3, T, T), BF),
            pltpu.VMEM((2, T, T), BF),
            pltpu.VMEM((2, T, T), BF),
            pltpu.VMEM((N_REP + 1, T, T), BF),
            pltpu.VMEM((3, 7, T, T), BF),
            pltpu.VMEM((3, 7, T, T), BF),
            pltpu.VMEM((2, NY, T, T), BF),
            pltpu.VMEM((2, NY, T, T), BF),
            pltpu.VMEM((2, T, T), BF),
            pltpu.VMEM((2, T, T), BF),
            pltpu.VMEM((T, 2 * T), F32),
            pltpu.VMEM((T // 2, 2 * T), F32),
            pltpu.VMEM((T // 2, 2 * T), F32),
            pltpu.VMEM((3, T // 8, 2 * T), F32),
            pltpu.VMEM((NY, T // 8, 2 * T), F32),
            pltpu.VMEM((NZL, T // 8, 2 * T), F32),
            pltpu.VMEM((NZH, T // 8, 2 * T), F32),
            pltpu.VMEM((2, NX, T // 8, 2 * T), F32),
            dma((7,)), dma((2,)), dma((3, 7)), dma((2, NY)), dma((N_WIDE,)),
            dma((NZH,)), dma((NZH,)), dma((NZH, 3)), dma((NZH, 3)), dma((2,)), dma((2,)),
            dma((23,)), dma((N_REP,)), dma((3, 7)), dma((3, 7)), dma((2, NY)), dma((2, NY)),
            dma((2,)), dma((2,)), dma((20,)), dma((24,)),
        ],
        compiler_params=pltpu.CompilerParams(
            collective_id=0, has_side_effects=True, vmem_limit_bytes=48 * 1024 * 1024
        ),
        name="graph_layer",
    )(*(
        pltpu.with_memory_space_constraint(value, pltpu.HBM)
        for value in (
            features, weight, cotangent,
            tile_values.reshape(N_WIDE, KT, T, T),
            tile_rows[0, 0].T, tile_counts.reshape(1, N_WIDE),
        )
    ))


def solution(mesh):
    in_specs = (
        P(("wide", "rep"), None),
        P(),
        P(("wide", "rep"), None),
        P("wide", "rep", None, None, None, None),
        P("wide", "rep", None, None),
        P("wide", "rep", None),
    )
    out_specs = (P(("wide", "rep"), None), P(), P(("wide", "rep"), None))
    return jax.shard_map(shards, mesh=mesh, in_specs=in_specs, out_specs=out_specs, check_vma=False)
```

time: 96.2 us -> 85 us (0.88)
  local copies, waits for them, and re-layouts: 7.79 us -> 1.9 us
  Pallas kernels: 86.2 us -> 82.4 us
  other arithmetic: 1.15 us -> 0 us
    unnamed x12 -> x3, local copies, waits for them, and re-layouts: 7.29 us -> 1.9 us
    pallas_call x1, Pallas kernels: 86.2 us -> 82.4 us  [shards(): pl.pallas_call(kernel, out_shape=shapes, in_specs=[hbm] * 6, out_specs=(v...]
where the time goes in v2:
time: 85 us; the launch traced here: 84.9 us
  Pallas kernels  82.4 us (97%)
  local copies, waits for them, and re-layouts  1.9 us (2%)
    pallas_call x1, Pallas kernels, shards(): pl.pallas_call(kernel, out_shape=shapes, in_specs=[hbm] * 6, out_specs=(v...  82.4 us
    unnamed x3, local copies, waits for them, and re-layouts  1.9 us

profile of v2, /device:TPU:1, one launch (start us, length us, event | category | flops | bytes accessed | tf_op | source)
XLA Modules:
  0.0 84.9 jit_solution(15055829961150466210)
XLA Ops:
  0.6 82.4 %graph_layer.1 = (bf16[128,256]{1,0:T(8,128)(2,1)S(1)}, f32[128,256]{1,0:T(8,128)S(1)}, bf16[128,128]{1,0:T(8,128)(2,1)S(1)}) custom-call(bf16[128,128]{1,0:T(8,128)(2,1)} %feat_hbm.1, bf16[128,256]{1,0:T(8,128)(2,1)} %weight_hbm.1, bf16[128,256]{1,0:T(8,128)(2,1)} %cot_hbm.1, bf16[32,4,128,128]{3,2,1,0:T(8,128)(2,1)} %bitcast.5, s32[4,32]{1,0:T(4,128)} %bitcast.6, ...), custom_call_target="tpu_custom_call" | custom-call | tf_op jit(solution)/shard_map/graph_layer/pallas_call | solution.py:603
  83.0 0.6 copy.12
  83.6 0.7 copy.13
  84.3 0.6 copy.14

commit v3 on v2

--- a/solution.py
+++ b/solution.py
@@ -34,7 +34,7 @@
     feat_hbm, weight_hbm, cot_hbm, tiles_hbm, rows_hbm, counts_hbm,
     out_ref, wgrad_ref, fgrad_ref,
     weight, cot, rows, counts, table_v, table, tiles, xs, tot, sib_s, sib_r, x_s, x_r, z_s, z_r, g, y_s, y_r, h_s, h_r, f_s, f_r,
-    w_t, w_r1, w_a, w_r2, w_c, w_d, w_e, w_o,
+    w_t, w_r, w_c, w_d, w_e, w_o,
     load_sems, ag_zs, ag_ys, ag_hs, ag_r, sib_ss, sib_rs, x_ss, x_rs, z_ss, z_rs,
     g_ss, g_rs, y_ss, y_rs, h_ss, h_rs, f_ss, f_rs, w_ss, w_rs,
 ):
@@ -80,8 +80,9 @@
     h_r[1] = jnp.zeros((NY, T, T), BF)
     f_r[1] = jnp.zeros((T, T), BF)
     barrier = pltpu.get_barrier_semaphore()
-    partners = [sibling]
-    partners += [dev(x=up(x, d, NX)) for d in range(1, NX)]
+    chips = [(dx, dc) for dx in range(NX) for dc in range(2) if dx or dc]
+    around = [dev(x=up(x, dx, NX), core=lax.rem(core + dc, 2)) for dx, dc in chips]
+    partners = list(around)
     partners += [dev(y=up(y, d, NY)) for d in range(1, NY)]
     partners += [dev(zl=up(zl, d, NZL)) for d in range(1, NZL)]
     partners += [dev(zh=up(zh, d, NZH)) for d in range(1, NZH)]
@@ -278,45 +279,57 @@
     g_send(5, mine, sibling)
 
     out_ref[...] = (hidden * sig).astype(BF)
-    w_t[...] = lax.dot_general(
+    term_of_weight = lax.dot_general(
         agg, grad_hidden, (((0,), (0,)), ((), ())), preferred_element_type=F32
     )
-    half = T // 2
-    chunk = half // NX
-    mine_half = pl.ds(pl.multiple_of(core * half, half), half)
-    other_half = pl.ds(pl.multiple_of((1 - core) * half, half), half)
-    send(w_t.at[other_half], w_r1, w_ss.at[0], w_rs.at[0], sibling)
-
-    for n in range(2):
-        r = up(zh, 2 - n, NZH) * (2 * NX) + x * 2 + core
+    for i in range(2):
+        for j in range(NX):
+            row = (i * NX + j) * (T // 8)
+            w_t[i, j] = term_of_weight[row:row + T // 8]
+    for n, (dx, dc) in enumerate(chips):
+        part_for = w_t.at[lax.rem(core + dc, 2), up(x, dx, NX)]
+        send(part_for, w_r.at[n], w_ss.at[n], w_rs.at[n], around[n])
+
+    early = (jnp.where(zh == 2, 1, 2), jnp.where(zh == 0, 1, 0))
+
+    def from_z(n):
+        r = early[n] * (2 * NX) + x * 2 + core
         wait_recv(g.at[r], g_rs.at[r])
         for m, dx in enumerate(X_ORDER):
             g_send(6 + 4 * n + m, r, dev(x=up(x, dx, NX)))
         g_send(6 + 4 * n + 3, r, sibling)
 
-    wait_recv(w_r1, w_rs.at[0])
-    w_a[...] = w_t[mine_half] + w_r1[...]
-
-    def chunk_of(v):
-        return pl.ds(pl.multiple_of(v * chunk, chunk), chunk)
-
-    for n, dx in enumerate(X_ORDER):
-        to = up(x, dx, NX)
-        send(w_a.at[chunk_of(to)], w_r2.at[n], w_ss.at[1 + n], w_rs.at[1 + n], dev(x=to))
-
-    for q in range(NZH):
+    def from_x(q, at):
         for n, dx in enumerate(X_ORDER):
-            r = up(zh, NZH - q, NZH) * (2 * NX) + up(x, NX - dx, NX) * 2 + core
+            r = at * (2 * NX) + up(x, NX - dx, NX) * 2 + core
             wait_recv(g.at[r], g_rs.at[r])
             g_send(14 + 3 * q + n, r, sibling)
 
-    w_sum = w_a[chunk_of(x)]
-    for n in range(3):
-        wait_recv(w_r2.at[n], w_rs.at[1 + n])
-        w_sum = w_sum + w_r2[n]
+    def spread_sum(buf, base, me, n):
+        for i in range(n):
+            @pl.when(me != i)
+            def _():
+                wait_recv(buf.at[i], w_rs.at[base + i])
+        value = buf[0]
+        for i in range(1, n):
+            value = value + buf[i]
+        return value
+
+    from_z(0)
+    w_sum = w_t[core, x]
+    for n in range(7):
+        wait_recv(w_r.at[n], w_rs.at[n])
+        w_sum = w_sum + w_r[n]
     w_c[y] = w_sum
     for n in range(1, NY):
-        send(w_c.at[y], w_c.at[y], w_ss.at[3 + n], w_rs.at[4 + y], dev(y=up(y, n, NY)))
+        send(w_c.at[y], w_c.at[y], w_ss.at[6 + n], w_rs.at[7 + y], dev(y=up(y, n, NY)))
+    from_z(1)
+    from_x(0, zh)
+    from_x(1, early[0])
+    w_d[zl] = spread_sum(w_c, 7, y, NY)
+    for n in range(1, NZL):
+        send(w_d.at[zl], w_d.at[zl], w_ss.at[13 + n], w_rs.at[15 + zl], dev(zl=up(zl, n, NZL)))
+    from_x(2, early[1])
 
     def sib_wait(n, carry):
         r = n * 2 + 1 - core
@@ -422,22 +435,9 @@
 
     outer_part(own_line)
 
-    def spread_sum(buf, base, me, n):
-        def wait_one(i, carry):
-            @pl.when(i != me)
-            def _():
-                wait_recv(buf.at[i], w_rs.at[base + i])
-            return carry
-
-        lax.fori_loop(0, n, wait_one, 0)
-        value = buf[0]
-        for i in range(1, n):
-            value = value + buf[i]
-        return value
-
-    w_d[zl] = spread_sum(w_c, 4, y, NY)
-    for n in range(1, NZL):
-        send(w_d.at[zl], w_d.at[zl], w_ss.at[10 + n], w_rs.at[12 + zl], dev(zl=up(zl, n, NZL)))
+    w_e[zh] = spread_sum(w_d, 15, zl, NZL)
+    for n in range(1, NZH):
+        send(w_e.at[zh], w_e.at[zh], w_ss.at[16 + n], w_rs.at[19 + zh], dev(zh=up(zh, n, NZH)))
 
     second_part(across)
 
@@ -453,9 +453,9 @@
 
     next_part(own_line)
 
-    w_e[zh] = spread_sum(w_d, 12, zl, NZL)
-    for n in range(1, NZH):
-        send(w_e.at[zh], w_e.at[zh], w_ss.at[13 + n], w_rs.at[16 + zh], dev(zh=up(zh, n, NZH)))
+    w_o[core, x] = spread_sum(w_e, 19, zh, NZH) * (1.0 / math.sqrt(N_WIDE * N_REP * T))
+    for n in range(7):
+        send(w_o.at[core, x], w_o.at[core, x], w_ss.at[19 + n], w_rs.at[22 + core * NX + x], around[n])
 
     second_part(own_line)
     z_send(0, across)
@@ -466,20 +466,6 @@
 
     value = whole(own_line)
 
-    w_own = spread_sum(w_e, 16, zh, NZH) * (1.0 / math.sqrt(N_WIDE * N_REP * T))
-    w_o[core, x] = w_own
-    for n in range(1, NX):
-        send(w_o.at[core, x], w_o.at[core, x], w_ss.at[15 + n], w_rs.at[19 + x], dev(x=up(x, n, NX)))
-
-    def gathered(i, carry):
-        @pl.when(i != x)
-        def _():
-            wait_recv(w_o.at[core, i], w_rs.at[19 + i])
-        return carry
-
-    lax.fori_loop(0, NX, gathered, 0)
-    send(w_o.at[core], w_o.at[core], w_ss.at[19], w_rs.at[23], sibling)
-
     wait_recv(f_r.at[0], f_rs.at[0])
     value = value + f_r[0].astype(F32)
 
@@ -489,7 +475,9 @@
 
     value = value + jnp.where(mid, 0.0, f_r[1].astype(F32))
     fgrad_ref[...] = value.T.astype(BF)
-    wait_recv(w_o.at[1 - core], w_rs.at[23])
+    for n, (dx, dc) in enumerate(chips):
+        i, j = lax.rem(core + dc, 2), up(x, dx, NX)
+        wait_recv(w_o.at[i, j], w_rs.at[22 + i * NX + j])
     wgrad_ref[...] = w_o[...].reshape(T, 2 * T)
 
     def settle(n, carry):
@@ -538,14 +526,12 @@
         return carry
 
     lax.fori_loop(0, 23, drain_g, 0)
-    wait_send(w_r1, w_ss.at[0])
 
     def drain_w(n, carry):
-        wait_send(w_r2.at[0], w_ss.at[n])
+        wait_send(w_r.at[0], w_ss.at[n])
         return carry
 
-    lax.fori_loop(1, 19, drain_w, 0)
-    wait_send(w_o.at[core], w_ss.at[19])
+    lax.fori_loop(0, 26, drain_w, 0)
 
 
 def rank_of(c):
@@ -628,10 +614,8 @@
             pltpu.VMEM((2, NY, T, T), BF),
             pltpu.VMEM((2, T, T), BF),
             pltpu.VMEM((2, T, T), BF),
-            pltpu.VMEM((T, 2 * T), F32),
-            pltpu.VMEM((T // 2, 2 * T), F32),
-            pltpu.VMEM((T // 2, 2 * T), F32),
-            pltpu.VMEM((3, T // 8, 2 * T), F32),
+            pltpu.VMEM((2, NX, T // 8, 2 * T), F32),
+            pltpu.VMEM((7, T // 8, 2 * T), F32),
             pltpu.VMEM((NY, T // 8, 2 * T), F32),
             pltpu.VMEM((NZL, T // 8, 2 * T), F32),
             pltpu.VMEM((NZH, T // 8, 2 * T), F32),
@@ -639,7 +623,7 @@
             dma((7,)), dma((2,)), dma((3, 7)), dma((2, NY)), dma((N_WIDE,)),
             dma((NZH,)), dma((NZH,)), dma((NZH, 3)), dma((NZH, 3)), dma((2,)), dma((2,)),
             dma((23,)), dma((N_REP,)), dma((3, 7)), dma((3, 7)), dma((2, NY)), dma((2, NY)),
-            dma((2,)), dma((2,)), dma((20,)), dma((24,)),
+            dma((2,)), dma((2,)), dma((26,)), dma((30,)),
         ],
         compiler_params=pltpu.CompilerParams(
             collective_id=0, has_side_effects=True, vmem_limit_bytes=48 * 1024 * 1024

time: 85 us -> 81.4 us (0.958)
  Pallas kernels: 82.4 us -> 78.7 us
    pallas_call x1, Pallas kernels: 82.4 us -> 78.7 us  [shards(): pl.pallas_call(kernel, out_shape=shapes, in_specs=[hbm] * 6, out_specs=(v...]
where the time goes in v3:
time: 81.4 us; the launch traced here: 81.3 us
  Pallas kernels  78.7 us (97%)
  local copies, waits for them, and re-layouts  1.9 us (2%)
    pallas_call x1, Pallas kernels, shards(): pl.pallas_call(kernel, out_shape=shapes, in_specs=[hbm] * 6, out_specs=(v...  78.7 us
    unnamed x3, local copies, waits for them, and re-layouts  1.9 us

profile of v3, /device:TPU:1, one launch (start us, length us, event | category | flops | bytes accessed | tf_op | source)
XLA Modules:
  0.0 81.3 jit_solution(15810919188177501019)
XLA Ops:
  0.6 78.7 %graph_layer.1 = (bf16[128,256]{1,0:T(8,128)(2,1)S(1)}, f32[128,256]{1,0:T(8,128)S(1)}, bf16[128,128]{1,0:T(8,128)(2,1)S(1)}) custom-call(bf16[128,128]{1,0:T(8,128)(2,1)} %feat_hbm.1, bf16[128,256]{1,0:T(8,128)(2,1)} %weight_hbm.1, bf16[128,256]{1,0:T(8,128)(2,1)} %cot_hbm.1, bf16[32,4,128,128]{3,2,1,0:T(8,128)(2,1)} %bitcast.5, s32[4,32]{1,0:T(4,128)} %bitcast.6, ...), custom_call_target="tpu_custom_call" | custom-call | tf_op jit(solution)/shard_map/graph_layer/pallas_call | solution.py:589
  79.4 0.6 copy.12
  80.0 0.7 copy.13
  80.7 0.6 copy.14

commit v4 on v3

--- a/solution.py
+++ b/solution.py
@@ -18,7 +18,7 @@
 STEPS = (
     [(0, 0)] + [(0, dy) for dy in NEAR] + [(2, 0), (1, 0), (3, 0)] + [(0, dy) for dy in FAR]
     + [(line, dy) for line in (2, 1, 3) for dy in NEAR]
-    + [(line, dy) for line in (1, 2, 3) for dy in FAR]
+    + [(line, dy) for line in (2, 1, 3) for dy in FAR]
 )
 
 
@@ -195,11 +195,6 @@
         have(other, 0)
 
     onward(across)
-
-    @pl.when(jnp.logical_not(mid))
-    def _():
-        onward(other)
-
     for dy in (-3, 3, 4):
         have(own_line, dy)
         z_pass(dy)
@@ -211,16 +206,20 @@
         have(pair, dy)
     work(15, STEPS[15:19])
 
-    @pl.when(mid)
-    def _():
-        have(other, -2)
-        have(other, 2)
-
-    have(other, -1)
-    have(other, 1)
+    for n, dy in enumerate(FAR):
+        have(across, dy)
+        c = block(across, dy)
+
+        @pl.when(mid)
+        def _():
+            send(xs.at[c], xs.at[c], ag_hs.at[2, n], ag_r.at[c], dev(zl=lines[pair]))
+
+    for dy in NEAR:
+        have(other, dy)
     work(19, STEPS[19:23])
-    for first, line in ((23, pair), (26, across), (29, other)):
-        for dy in (-3, 3, 4):
+    work(23, STEPS[23:26])
+    for first, line in ((26, pair), (29, other)):
+        for dy in FAR:
             have(line, dy)
         work(first, STEPS[first:first + 3])
 
@@ -500,12 +499,22 @@
 
         @pl.when(jnp.logical_not(mid))
         def _():
+            wait_send(y_s.at[2, n], y_ss.at[2, n])
+
+        return carry
+
+    lax.fori_loop(0, 7, drain, 0)
+
+    @pl.when(mid)
+    def _():
+        for n in range(len(FAR)):
+            wait_send(xs.at[0], ag_hs.at[2, n])
+
+    @pl.when(jnp.logical_not(mid))
+    def _():
+        for n in range(4):
             wait_send(xs.at[0], ag_ys.at[2, n])
-            wait_send(y_s.at[2, n], y_ss.at[2, n])
-
-        return carry
-
-    lax.fori_loop(0, 7, drain, 0)
+
     wait_send(xs.at[0], ag_zs.at[0])
     wait_send(f_s.at[0], f_ss.at[0])
 
@@ -620,7 +629,7 @@
             pltpu.VMEM((NZL, T // 8, 2 * T), F32),
             pltpu.VMEM((NZH, T // 8, 2 * T), F32),
             pltpu.VMEM((2, NX, T // 8, 2 * T), F32),
-            dma((7,)), dma((2,)), dma((3, 7)), dma((2, NY)), dma((N_WIDE,)),
+            dma((7,)), dma((2,)), dma((3, 7)), dma((3, NY)), dma((N_WIDE,)),
             dma((NZH,)), dma((NZH,)), dma((NZH, 3)), dma((NZH, 3)), dma((2,)), dma((2,)),
             dma((23,)), dma((N_REP,)), dma((3, 7)), dma((3, 7)), dma((2, NY)), dma((2, NY)),
             dma((2,)), dma((2,)), dma((26,)), dma((30,)),

time: 81.4 us -> 81.5 us (level)
  no operation moved by 1% of the time
where the time goes in v4:
time: 81.5 us; the launch traced here: 81.4 us
  Pallas kernels  78.9 us (97%)
  local copies, waits for them, and re-layouts  1.9 us (2%)
    pallas_call x1, Pallas kernels, shards(): pl.pallas_call(kernel, out_shape=shapes, in_specs=[hbm] * 6, out_specs=(v...  78.9 us
    unnamed x3, local copies, waits for them, and re-layouts  1.9 us

profile of v4, /device:TPU:1, one launch (start us, length us, event | category | flops | bytes accessed | tf_op | source)
XLA Modules:
  0.0 81.4 jit_solution(17907449916356593565)
XLA Ops:
  0.6 78.9 %graph_layer.1 = (bf16[128,256]{1,0:T(8,128)(2,1)S(1)}, f32[128,256]{1,0:T(8,128)S(1)}, bf16[128,128]{1,0:T(8,128)(2,1)S(1)}) custom-call(bf16[128,128]{1,0:T(8,128)(2,1)} %feat_hbm.1, bf16[128,256]{1,0:T(8,128)(2,1)} %weight_hbm.1, bf16[128,256]{1,0:T(8,128)(2,1)} %cot_hbm.1, bf16[32,4,128,128]{3,2,1,0:T(8,128)(2,1)} %bitcast.5, s32[4,32]{1,0:T(4,128)} %bitcast.6, ...), custom_call_target="tpu_custom_call" | custom-call | tf_op jit(solution)/shard_map/graph_layer/pallas_call | solution.py:598
  79.5 0.6 copy.12
  80.1 0.7 copy.13
  80.8 0.6 copy.14
